TPU v7x, 512 devices: a whole 4x8x8 slice. The times are simulated.
512 devices in a mesh: tile: 32 (over x, z), pair: 16 (over y, core).
Axes of the slice: x: 4, y: 8, z: 8, core: 2. Of those that a mesh axis runs over, the one named last changes fastest.
Arguments:
- samples: bfloat16 [256, 512, 1024], P('tile', 'pair'), may hold values from -48 to 48
- pair_list: int32 [1024, 2], P('tile'), may hold values from 0 to 255, as said below
- taper_bins: int32 [1024], P(('tile', 'pair')), may hold values from 0 to 7
Outputs:
- covariance: bfloat16 [1024, 1024, 1024], P(('tile', 'pair'))
Inputs may be any that keep to these rules, and one draw needn't show every extreme that they name: `pair_list`: pairs are listed by groups of 32 rows; the first tile of every pair of group k is one of tiles k * 8 to (k + 1) * 8 - 1. The second tile lies within 2 tiles of the first, counted cyclically around the band of 256 tiles; in every group some pair reaches 2 tiles down from the group's first tile and some 2 tiles up from its last.
All inputs are finite; a program needn't handle non-finite values.
Results may differ from a plain program's by a relative error of at most 0.0053.
Values may be sent and summed in bfloat16 or wider, within the bound.
A program may use at most 64 MiB of HBM per device.

v0:
```python
import jax
import jax.numpy as jnp
from jax import lax
from jax.sharding import PartitionSpec as P

REACH = 2
NBINS = 8


def extended_2(cells, sides, width):
    for axis, dim in sides:
        count = lax.axis_size(axis)
        head = lax.slice_in_dim(cells, 0, width, axis=dim)
        tail = lax.slice_in_dim(cells, cells.shape[dim] - width, cells.shape[dim], axis=dim)
        cells = jnp.concatenate(
            [
                lax.ppermute(tail, axis, [(i, (i + 1) % count) for i in range(count)]),
                cells,
                lax.ppermute(head, axis, [((i + 1) % count, i) for i in range(count)]),
            ],
            axis=dim,
        )
    return cells


def local(samples, pair_list, taper_bins):
    tile_count, block_samples, pixels = samples.shape
    span_sums = lax.psum(jnp.sum(samples, axis=1, dtype=jnp.float32), "pair")
    pair_groups = lax.axis_size("pair")
    sample_count = block_samples * pair_groups
    tile_mean = span_sums / sample_count
    centered = (samples.astype(jnp.float32) - tile_mean[:, None, :]).astype(jnp.bfloat16)
    extended = extended_2(centered, (("tile", 0),), REACH)
    band_tiles = tile_count * lax.axis_size("tile")
    start_tile = lax.axis_index("tile") * tile_count
    local_pairs = (pair_list - start_tile + REACH + band_tiles) % band_tiles
    per_device = pair_list.shape[0] // pair_groups
    own_pairs = lax.dynamic_slice_in_dim(
        local_pairs, lax.axis_index("pair") * per_device, per_device, 0
    )
    taper_weight = 1.0 - taper_bins.astype(jnp.float32) / NBINS
    factor = taper_weight / jnp.float32(sample_count - 1)
    contract = (((1,), (1,)), ((0,), (0,)))
    block_rows = lax.all_gather(extended, "pair", axis=1, tiled=True)
    left_rows = jnp.take(block_rows, own_pairs[:, 0], axis=0)
    right_rows = jnp.take(block_rows, own_pairs[:, 1], axis=0)
    gram_sum = lax.dot_general(left_rows, right_rows, contract, preferred_element_type=jnp.float32)
    return (gram_sum * factor[:, None, None]).astype(jnp.bfloat16)


def solution(mesh):
    in_specs = (P("tile", "pair", None), P("tile", None), P(("tile", "pair")))
    out_specs = P(("tile", "pair"), None, None)
    return jax.shard_map(local, mesh=mesh, in_specs=in_specs, out_specs=out_specs, check_vma=False)
```

profile of v0, /device:TPU:1, one launch (start us, length us, event | category | flops | bytes accessed | tf_op | source)
XLA Modules:
  0.0 176.3 jit_solution(5330625359980897423)
XLA Ops:
  6.5 0.0 all-gather.2.cloned.1.call-start
  6.5 1.2 convert_reduce_fusion
  7.7 0.0 copy-start
  7.7 0.0 copy-start.1
  7.7 49.0 %psum.7 = f32[8,1024]{1,0:T(8,128)S(1)} all-reduce(f32[8,1024]{1,0:T(8,128)S(1)} %convert_reduce_fusion), channel_id=1, replica_groups=mesh['tile'=32,'pair'=16] {'pair'}, use_global_device_ids=true, to_apply=%region_1.0 | all-reduce | flops 8192 | bytes 65536 | tf_op jit(solution)/shard_map/psum | solution.py:28
  56.8 1.2 fusion.4
  58.0 1.9 %collective-permute-start = (bf16[2,32,1024]{2,1,0:T(8,128)(2,1)S(1)}, bf16[2,32,1024]{2,1,0:T(8,128)(2,1)S(1)}, u32[]{:S(2)}, u32[]{:S(2)}) collective-permute-start(bf16[2,32,1024]{2,1,0:T(8,128)(2,1)S(1)} %get-tuple-element.10), channel_id=1, source_target_pairs={{0,16},{16,32},{32,48},{48,64},{64,80},{80,96},{96,112},{112,128},... | collective-permute-start | bytes 393224 | tf_op jit(solution)/shard_map/ppermute | solution.py:17
  59.9 10.3 %collective-permute-start.1 = (bf16[2,32,1024]{2,1,0:T(8,128)(2,1)S(1)}, bf16[2,32,1024]{2,1,0:T(8,128)(2,1)S(1)}, u32[]{:S(2)}, u32[]{:S(2)}) collective-permute-start(bf16[2,32,1024]{2,1,0:T(8,128)(2,1)S(1)} %get-tuple-element.11), channel_id=1, source_target_pairs={{16,0},{32,16},{48,32},{64,48},{80,64},{96,80},{112,96},{128,112},... | collective-permute-start | bytes 393224 | tf_op jit(solution)/shard_map/ppermute | solution.py:19
  70.2 0.4 collective-permute-done
  70.6 1.5 collective-permute-done.1
  72.1 1.0 pad_maximum_fusion
  73.1 0.0 all-gather.2.cloned.1.call-update
  73.1 0.0 copy-done
  73.1 0.1 constant_dynamic-slice_fusion
  73.2 0.0 copy-done.1
  73.2 78.3 %all-gather.2.cloned.1.call-done = bf16[12,512,1024]{2,1,0:T(8,128)(2,1)} async-done(((bf16[12,32,1024]{2,1,0:T(8,128)(2,1)}), bf16[12,512,1024]{2,1,0:T(8,128)(2,1)}) %all-gather.2.cloned.1.call-update) | async-done | bytes 12582928 | tf_op jit(solution)/shard_map/all_gather | solution.py:44
  151.6 5.3 %gather_fusion = bf16[2,512,1024]{2,1,0:T(8,128)(2,1)S(1)} fusion(bf16[12,512,1024]{2,1,0:T(8,128)(2,1)} %all-gather.2.cloned.1.call-done, s32[1024]{0:T(1024)S(1)} %get-tuple-element.15), kind=kCustom, calls=%fused_computation.clone | custom fusion | bytes 4194312 | tf_op jit(solution)/shard_map/jit(_take)/gather | solution.py:45
  156.8 6.6 %gather_fusion.1 = bf16[2,512,1024]{2,1,0:T(8,128)(2,1)} fusion(bf16[12,512,1024]{2,1,0:T(8,128)(2,1)} %all-gather.2.cloned.1.call-done, s32[1024]{0:T(1024)S(1)} %get-tuple-element.14), kind=kCustom, calls=%fused_computation.1.clone | custom fusion | bytes 4194312 | tf_op jit(solution)/shard_map/jit(_take)/gather | solution.py:46
  163.4 6.1 %multiply_convert_fusion = bf16[2,1024,1024]{2,1,0:T(8,128)(2,1)} fusion(f32[2]{0:T(128)S(1)} %subtract_multiply_fusion, bf16[2,512,1024]{2,1,0:T(8,128)(2,1)} %gather_fusion.1, bf16[2,512,1024]{2,1,0:T(8,128)(2,1)S(1)} %gather_fusion, pred[2]{0:T(512)(128)(4,1)S(1)} %get-tuple-element.12, pred[2]{0:T(512)(128)(4,1)S(1)} %get-tuple-element.6), kind=kOutput, calls=%fused_computation.2 | convolution fusion | flops 2153775104 | bytes 8388620 | tf_op jit(solution)/shard_map/dot_general | solution.py:47
  (6 shorter events, 0.1 us)
Async XLA Ops:
  6.5 145.0 %all-gather.2.cloned.1.call-start = ((), (), s32[]{:S(2)}) async-start(), calls=%async_computation | async-start | bytes 13369344 | tf_op jit(solution)/shard_map/all_gather | solution.py:44
  7.7 65.4 %copy-start = (s32[32,2]{0,1:T(2,128)S(1)}, s32[32,2]{0,1:T(2,128)}, u32[]{:S(2)}) copy-start(s32[32,2]{0,1:T(2,128)} %param.6) | copy-start | bytes 772
  7.7 65.5 %copy-start.1 = (s32[2]{0:T(128)S(1)}, s32[2]{0:T(128)}, u32[]{:S(2)}) copy-start(s32[2]{0:T(128)} %param.7) | copy-start | bytes 28
  58.0 12.6 %collective-permute-start = (bf16[2,32,1024]{2,1,0:T(8,128)(2,1)S(1)}, bf16[2,32,1024]{2,1,0:T(8,128)(2,1)S(1)}, u32[]{:S(2)}, u32[]{:S(2)}) collective-permute-start(bf16[2,32,1024]{2,1,0:T(8,128)(2,1)S(1)} %get-tuple-element.10), channel_id=1, source_target_pairs={{0,16},{16,32},{32,48},{48,64},{64,80},{80,96},{96,112},{112,128},... | collective-permute-start | bytes 393224 | tf_op jit(solution)/shard_map/ppermute | solution.py:17
  59.9 12.2 %collective-permute-start.1 = (bf16[2,32,1024]{2,1,0:T(8,128)(2,1)S(1)}, bf16[2,32,1024]{2,1,0:T(8,128)(2,1)S(1)}, u32[]{:S(2)}, u32[]{:S(2)}) collective-permute-start(bf16[2,32,1024]{2,1,0:T(8,128)(2,1)S(1)} %get-tuple-element.11), channel_id=1, source_target_pairs={{16,0},{32,16},{48,32},{64,48},{80,64},{96,80},{112,96},{128,112},... | collective-permute-start | bytes 393224 | tf_op jit(solution)/shard_map/ppermute | solution.py:19
Sparse Core Ops, SparseCore 0:
  73.2 78.2 all-gather.1
where the time goes:
time: 177 us; the launch traced here: 176 us
  waiting for transfers between devices  80.2 us (45%)
  blocking collectives  49 us (28%)
  between operations  13.5 us (8%)
  starting transfers between devices  12.2 us (7%)
  local copies, waits for them, and re-layouts  12 us (7%)
  matrix products  6.07 us (3%)
  other arithmetic  3.34 us (2%)
    all_gather x1, waiting for transfers between devices, local(): block_rows = lax.all_gather(extended, 'pair', axis=1, tiled=True)  78.3 us
    psum x1, blocking collectives, local(): span_sums = lax.psum(jnp.sum(samples, axis=1, dtype=jnp.float32), 'pair')  49 us
    ppermute x1, starting transfers between devices, extended_2(): lax.ppermute(head, axis, [((i + 1) % count, i) for i in range(count)])  10.3 us
    gather x1, local copies, waits for them, and re-layouts, local(): right_rows = jnp.take(block_rows, own_pairs[:, 1], axis=0)  6.6 us
    dot_general x1, matrix products, local(): lax.dot_general(left_rows, right_rows, contract, preferred_element_type=j...  6.07 us
    gather x1, local copies, waits for them, and re-layouts, local(): left_rows = jnp.take(block_rows, own_pairs[:, 0], axis=0)  5.25 us
  transfers between devices with their start and end apart: 3, of which 3 were waited for; matrix products, arithmetic and copies ran while one was open for 0% of the time, Pallas kernels for 0%

commit v1 on v0

v1 whole, which is shorter than its diff:
```python
import functools

import jax
import jax.numpy as jnp
from jax import lax
from jax.experimental import pallas as pl
from jax.experimental.pallas import tpu as pltpu
from jax.sharding import PartitionSpec as P

REACH = 2
NBINS = 8
MESH = pl.DeviceIdType.MESH

INNER = slice(0, 4)
ENDS = slice(4, 8)
LAST = slice(4, 6)
FIRST = slice(6, 8)
FROM_PREV = slice(8, 10)
FROM_NEXT = slice(10, 12)
HALO = slice(8, 12)
SLOTS = 12


def slot_of(tile, start, band):
    rel = lax.rem(tile - start + REACH + band, band)
    rel = jnp.clip(rel, 0, SLOTS - 1)
    return jnp.where(rel < 2, rel + 8, jnp.where(rel < 4, rel + 4, jnp.where(rel < 10, rel - 4, rel)))


def gather_kernel(plan, pair_ref, samples_ref, acc_ref, last_ref, sum_ref, *scratch):
    tiles, chips, steps, rows, pixels, per_device = plan
    chunks = 2 * steps + 1
    mine, theirs = scratch[:chunks], scratch[chunks : 2 * chunks]
    u_ref, shift_ref, send_sem, recv_sem, local_sem = scratch[2 * chunks :]
    half = rows // 2
    right_way = [0] + [2 * s - 1 for s in range(1, steps + 1)]
    left_way = [0] + [2 * s for s in range(1, steps + 1)]

    t, p = lax.axis_index("tile"), lax.axis_index("pair")
    group = 2 * chips
    above, below = (lax.rem(t + 1, tiles), p), (lax.rem(t + tiles - 1, tiles), p)
    right, left = (t, lax.rem(p + 2, group)), (t, lax.rem(p + group - 2, group))
    other = (t, p + 1 - 2 * lax.rem(p, 2))

    count = [0]
    sent = []

    def send(src, dst, device):
        k = count[0]
        count[0] += 1
        copy = pltpu.make_async_remote_copy(
            src_ref=src, dst_ref=dst, send_sem=send_sem.at[k], recv_sem=recv_sem.at[k],
            device_id=device, device_id_type=MESH,
        )
        copy.start()
        sent.append(copy)
        return copy

    fills = []
    for k, (lo, hi, slots) in enumerate(((0, 2, FIRST), (6, 8, LAST), (2, 6, INNER))):
        fill = pltpu.make_async_copy(samples_ref.at[lo:hi], mine[0].at[slots], local_sem.at[k])
        fill.start()
        fills.append(fill)
    barrier = pltpu.get_barrier_semaphore()
    for device in (right, left, above, below, other):
        pl.semaphore_signal(barrier, inc=1, device_id=device, device_id_type=MESH)
    pl.semaphore_wait(barrier, 5)
    for fill in fills:
        fill.wait()

    def forward(step, part):
        if step == steps:
            return (None, None)
        r, l = right_way[step], left_way[step]
        r2, l2 = right_way[step + 1], left_way[step + 1]
        if step + 1 == steps:
            return (
                send(mine[r].at[part, 0:half], mine[r2].at[part], right),
                send(mine[l].at[part, half:rows], mine[l2].at[part], left),
            )
        return (
            send(mine[r].at[part], mine[r2].at[part], right),
            send(mine[l].at[part], mine[l2].at[part], left),
        )

    def ends_out(chunk):
        return (
            send(mine[chunk].at[LAST], mine[chunk].at[FROM_PREV], above),
            send(mine[chunk].at[FIRST], mine[chunk].at[FROM_NEXT], below),
        )

    def across(chunk, part):
        return send(mine[chunk].at[part], theirs[chunk].at[part], other)

    def of_step(step):
        return [0] if step == 0 else [right_way[step], left_way[step]]

    start, band = t * 8, tiles * 8

    def load(step, put):
        for q in range(per_device):
            for side in range(2):
                slot = slot_of(pair_ref[p * per_device + q, side], start, band)
                row = 0
                for chunk in of_step(step):
                    for held in (mine[chunk], theirs[chunk]):
                        put(q, side, row, held[slot].astype(jnp.float32))
                        row += held.shape[1]

    def work(step):
        depth = sum(2 * mine[chunk].shape[1] for chunk in of_step(step))
        if step == 0:
            totals = {}

            def add(q, side, row, values):
                total = jnp.sum(values, axis=0, keepdims=True)
                totals[q, side] = total if row == 0 else totals[q, side] + total

            load(0, add)
            for (q, side), total in totals.items():
                shift_ref[2 * q + side] = total * (1.0 / depth)
        final = step == steps
        sums = {}

        def put(q, side, row, values):
            u = (values - shift_ref[2 * q + side]).astype(jnp.bfloat16)
            into = last_ref if final else u_ref
            into[2 * q + side, pl.ds(row, values.shape[0]), :] = u
            total = jnp.sum(u.astype(jnp.float32), axis=0, keepdims=True)
            sums[q, side] = total if row == 0 else sums[q, side] + total

        load(step, put)
        for (q, side), total in sums.items():
            k = 2 * q + side
            sum_ref[k] = total if step == 0 else sum_ref[k] + total
        if final:
            return
        block = min(256, pixels)
        per_pair = pixels // block

        def body(i, _):
            q, m = lax.div(i, per_pair), pl.multiple_of(lax.rem(i, per_pair) * block, block)
            gram = lax.dot_general(
                u_ref[2 * q, 0:depth, pl.ds(m, block)], u_ref[2 * q + 1, 0:depth, :],
                (((0,), (0,)), ((), ())), preferred_element_type=jnp.float32,
            )
            if step == 0:
                acc_ref[q, pl.ds(m, block), :] = gram
            else:
                acc_ref[q, pl.ds(m, block), :] += gram
            return 0

        lax.fori_loop(0, per_device * per_pair, body, 0)

    ring = {}
    halos = {}
    cross = {}
    ring[0, 0] = forward(0, ENDS)
    halos[0] = ends_out(0)
    ring[0, 1] = forward(0, INNER)
    cross[0] = [across(0, ENDS), across(0, INNER)]

    def halo_across(step):
        for chunk in of_step(step):
            for copy in halos[chunk]:
                copy.wait_recv()
            cross[chunk].append(across(chunk, HALO))

    def arrive(step, part, index):
        for chunk, copy in zip(of_step(step), ring[step - 1, index]):
            copy.wait_recv()
        ring[step, index] = forward(step, part)
        if index == 0:
            for chunk in of_step(step):
                halos[chunk] = ends_out(chunk)
                cross[chunk] = []
        for chunk in of_step(step):
            cross[chunk].append(across(chunk, part))

    def ready(step):
        for chunk in of_step(step):
            for copy in cross[chunk]:
                copy.wait_recv()

    halo_across(0)
    for step in range(1, steps + 1):
        arrive(step, ENDS, 0)
        if step == steps:
            ready(step - 1)
            work(step - 1)
        else:
            halo_across(step)
        arrive(step, INNER, 1)
        if step == steps:
            halo_across(step)
        else:
            ready(step - 1)
            work(step - 1)
    ready(steps)
    work(steps)
    for copy in sent:
        copy.wait_send()


def finish_kernel(plan, bins_ref, acc_ref, last_ref, sum_ref, out_ref, stage, sem):
    samples, pixels, per_device = plan
    block = min(256, pixels)
    copies = []
    for q in range(per_device):
        weight = 1.0 - jnp.full((1, pixels), bins_ref[q], jnp.int32).astype(jnp.float32) / NBINS
        factor = weight / jnp.float32(samples - 1)
        total_a, total_b = sum_ref[2 * q], sum_ref[2 * q + 1] * (1.0 / samples)
        for m in range(0, pixels, block):
            rows = slice(m, m + block)
            gram = acc_ref[q, rows, :] + lax.dot_general(
                last_ref[2 * q, :, rows], last_ref[2 * q + 1], (((0,), (0,)), ((), ())),
                preferred_element_type=jnp.float32,
            )
            column = jnp.transpose(total_a[:, rows])
            stage[q, rows, :] = ((gram - column * total_b) * factor).astype(jnp.bfloat16)
            copy = pltpu.make_async_copy(stage.at[q, rows], out_ref.at[q, rows], sem.at[len(copies)])
            copy.start()
            copies.append(copy)
    for copy in copies:
        copy.wait()


def local(tiles, group, samples, pair_list, taper_bins):
    own_tiles, rows, pixels = samples.shape
    chips = group // 2
    steps = chips // 2
    per_device = taper_bins.shape[0]
    total_rows = rows * group
    plan = (tiles, chips, steps, rows, pixels, per_device)
    chunk_rows = [rows] * (2 * steps - 1) + [rows // 2] * 2
    chunks = [pltpu.VMEM((SLOTS, r, pixels), jnp.bfloat16) for r in chunk_rows]
    n_copies = 2 * 2 * steps + (2 + 3) * len(chunks)
    last_rows = 2 * rows
    acc, last, sums = pl.pallas_call(
        functools.partial(gather_kernel, plan),
        out_shape=(
            pltpu.VMEM((per_device, pixels, pixels), jnp.float32),
            pltpu.VMEM((2 * per_device, last_rows, pixels), jnp.bfloat16),
            pltpu.VMEM((2 * per_device, 1, pixels), jnp.float32),
        ),
        in_specs=[pl.BlockSpec(memory_space=pltpu.SMEM), pl.BlockSpec(memory_space=pl.ANY)],
        out_specs=[pl.BlockSpec(memory_space=pltpu.VMEM)] * 3,
        scratch_shapes=[
            *chunks,
            *chunks,
            pltpu.VMEM((2 * per_device, 4 * rows, pixels), jnp.bfloat16),
            pltpu.VMEM((2 * per_device, 1, pixels), jnp.float32),
            pltpu.SemaphoreType.DMA((n_copies,)),
            pltpu.SemaphoreType.DMA((n_copies,)),
            pltpu.SemaphoreType.DMA((3,)),
        ],
        compiler_params=pltpu.CompilerParams(
            collective_id=0, has_side_effects=True, vmem_limit_bytes=36 * 2**20
        ),
        name="gather_and_sum",
    )(pair_list, samples)
    return pl.pallas_call(
        functools.partial(finish_kernel, (total_rows, pixels, per_device)),
        out_shape=jax.ShapeDtypeStruct((per_device, pixels, pixels), jnp.bfloat16),
        in_specs=[pl.BlockSpec(memory_space=pltpu.SMEM)] + [pl.BlockSpec(memory_space=pltpu.VMEM)] * 3,
        out_specs=pl.BlockSpec(memory_space=pl.ANY),
        scratch_shapes=[
            pltpu.VMEM((per_device, pixels, pixels), jnp.bfloat16),
            pltpu.SemaphoreType.DMA((per_device * max(1, pixels // 256),)),
        ],
        compiler_params=pltpu.CompilerParams(vmem_limit_bytes=36 * 2**20),
        name="finish",
    )(taper_bins, acc, last, sums)


def solution(mesh):
    in_specs = (P("tile", "pair", None), P("tile", None), P(("tile", "pair")))
    out_specs = P(("tile", "pair"), None, None)
    body = functools.partial(local, mesh.shape["tile"], mesh.shape["pair"])
    return jax.shard_map(body, mesh=mesh, in_specs=in_specs, out_specs=out_specs, check_vma=False)
```

time: 177 us -> 72.4 us (0.41)
  waiting for transfers between devices: 80.2 us -> 0 us
  Pallas kernels: 0 us -> 69.7 us
  blocking collectives: 49 us -> 0 us
  between operations: 13.5 us -> 0.02 us
  starting transfers between devices: 12.2 us -> 0 us
  local copies, waits for them, and re-layouts: 12 us -> 2.45 us
  matrix products: 6.07 us -> 0 us
  other arithmetic: 3.34 us -> 0 us
    all_gather x1 -> x0, waiting for transfers between devices: 78.3 us -> none  [local(): block_rows = lax.all_gather(extended, 'pair', axis=1, tiled=True)]
    pallas_call x0 -> x2, Pallas kernels: none -> 69.7 us  [the longest x1 65.8 us: local(): pl.pallas_call(functools.partial(gather_kernel, plan), out_shape=(pltpu.V...]
    psum x1 -> x0, blocking collectives: 49 us -> none  [local(): span_sums = lax.psum(jnp.sum(samples, axis=1, dtype=jnp.float32), 'pair')]
    ppermute x2 -> x0, starting transfers between devices: 12.2 us -> none  [the longest x1 10.3 us: extended_2(): lax.ppermute(head, axis, [((i + 1) % count, i) for i in range(count)])]
    gather x2 -> x0, local copies, waits for them, and re-layouts: 11.9 us -> none  [the longest x1 6.6 us: local(): right_rows = jnp.take(block_rows, own_pairs[:, 1], axis=0)]
    dot_general x1 -> x0, matrix products: 6.07 us -> none  [local(): lax.dot_general(left_rows, right_rows, contract, preferred_element_type=j...]
    unnamed x4 -> x5, local copies, waits for them, and re-layouts: 0.01 us -> 2.45 us
    ppermute x2 -> x0, waiting for transfers between devices: 1.93 us -> none  [the longest x1 1.51 us: extended_2(): lax.ppermute(head, axis, [((i + 1) % count, i) for i in range(count)])]
  transfers between devices with their start and end apart: 3 -> 0, of which waited for: 3 -> 0; matrix products, arithmetic and copies ran while one was open for 0% -> 0% of each run, Pallas kernels for 0% -> 0%
where the time goes in v1:
time: 72.4 us; the launch traced here: 72.2 us
  Pallas kernels  69.7 us (96%)
  local copies, waits for them, and re-layouts  2.45 us (3%)
    pallas_call x1, Pallas kernels, local(): pl.pallas_call(functools.partial(gather_kernel, plan), out_shape=(pltpu.V...  65.8 us
    pallas_call x1, Pallas kernels, local(): pl.pallas_call(functools.partial(finish_kernel, (total_rows, pixels, per_...  3.92 us
    unnamed x5, local copies, waits for them, and re-layouts  2.45 us

profile of v1, /device:TPU:1, one launch (start us, length us, event | category | flops | bytes accessed | tf_op | source)
XLA Modules:
  0.0 72.2 jit_solution(5091174666402360915)
XLA Ops:
  0.0 0.8 %copy.4.pair_ref = s32[32,2]{1,0:T(8,128)S(1)} copy(s32[32,2]{0,1:T(2,128)} %param.4) | data formatting | bytes 512 | tf_op args[1]
  0.8 0.0 copy-start
  0.8 1.0 %copy-done = bf16[8,32,1024]{2,1,0:T(8,128)(2,1)S(1)} copy-done((bf16[8,32,1024]{2,1,0:T(8,128)(2,1)S(1)}, bf16[8,32,1024]{2,1,0:T(8,128)(2,1)}, u32[]{:S(2)}) %copy-start) | copy-done | bytes 524312
  1.8 65.8 %gather_and_sum.1 = (f32[2,1024,1024]{2,1,0:T(8,128)S(1)}, bf16[4,64,1024]{2,1,0:T(8,128)(2,1)S(1)}, f32[4,1,1024]{2,1,0:T(1,128)S(1)}) custom-call(s32[32,2]{1,0:T(8,128)S(1)} %copy.4.pair_ref, bf16[8,32,1024]{2,1,0:T(8,128)(2,1)S(1)} %copy-done), custom_call_target="tpu_custom_call" | custom-call | tf_op jit(solution)/shard_map/gather_and_sum/pallas_call | solution.py:239
  67.6 0.0 copy-start.1
  67.6 0.6 copy-done.1
  68.3 3.9 %finish.1 = bf16[2,1024,1024]{2,1,0:T(8,128)(2,1)} custom-call(s32[2]{0:T(128)S(1)} %copy-done.1, f32[2,1024,1024]{2,1,0:T(8,128)S(1)} %get-tuple-element.8.acc_ref, bf16[4,64,1024]{2,1,0:T(8,128)(2,1)S(1)} %get-tuple-element.9.last_ref, f32[4,1,1024]{2,1,0:T(1,128)S(1)} %get-tuple-element.10.sum_ref), custom_call_target="tpu_custom_call" | custom-call | tf_op jit(solution)/shard_map/finish/pallas_call | solution.py:262
Async XLA Ops:
  0.8 1.0 %copy-start = (bf16[8,32,1024]{2,1,0:T(8,128)(2,1)S(1)}, bf16[8,32,1024]{2,1,0:T(8,128)(2,1)}, u32[]{:S(2)}) copy-start(bf16[8,32,1024]{2,1,0:T(8,128)(2,1)} %samples_ref.1) | copy-start | bytes 1572868
  67.6 0.7 copy-start.1

commit v2 on v1

v2 whole, which is shorter than its diff:
```python
import functools

import jax
import jax.numpy as jnp
from jax import lax
from jax.experimental import pallas as pl
from jax.experimental.pallas import tpu as pltpu
from jax.sharding import PartitionSpec as P

REACH = 2
NBINS = 8
LINE = 8
MESH = pl.DeviceIdType.MESH

PARTS = {"c": slice(0, 2), "d": slice(2, 4), "e": slice(4, 8)}
LAST, FIRST = slice(4, 6), slice(6, 8)
FROM_BELOW, FROM_ABOVE = slice(8, 10), slice(10, 12)
SLOTS = 12


def schedule(steps):
    order = ["e0", "u0", "c0", "e1", "d0", "s0", "e2", "v0"]
    for step in range(1, steps):
        order += [f"c{step}", f"d{step}"]
        if step == 1:
            order += ["x0", "w0", "e3", "x1", "w1"]
        else:
            order += [f"x{step}", f"e{step + 2}", f"w{step}"]
    order += [f"c{steps}", f"d{steps}", f"x{steps}", f"w{steps}"]
    return [(o[0], int(o[1:])) for o in order if o[0] != "e" or int(o[1:]) <= steps]


def slot_of(tile, start, band):
    rel = jnp.clip(lax.rem(tile - start + REACH + band, band), 0, SLOTS - 1)
    return jnp.where(rel < 2, rel + 8, jnp.where(rel < 4, rel + 4, jnp.where(rel < 10, rel - 4, rel)))


def gather_kernel(plan, pairs_ref, bins_ref, samples_ref, acc_ref, last_ref, sum_ref, factor_ref, *scratch):
    tiles, chips, steps, rows, pixels, per_device = plan
    chunks = 2 * steps + 1
    mine, theirs = scratch[:chunks], scratch[chunks : 2 * chunks]
    u_ref, shift_ref, pairs, bins, send_sem, recv_sem, local_sem, ready_sem = scratch[2 * chunks :]
    half = rows // 2

    def of_step(step):
        return [0] if step == 0 else [2 * step - 1, 2 * step]

    t, p = lax.axis_index("tile"), lax.axis_index("pair")
    group = 2 * chips
    core = lax.rem(p, 2)
    above, below = (lax.rem(t + 1, tiles), p), (lax.rem(t + tiles - 1, tiles), p)
    right, left = (t, lax.rem(p + 2, group)), (t, lax.rem(p + group - 2, group))
    other = (t, p + 1 - 2 * core)

    turned_below = lax.rem(t, LINE) == 0
    turned_above = lax.rem(lax.rem(t + 1, tiles), LINE) == 0
    first_core = core == 0

    def greet(sem, device):
        pl.semaphore_signal(sem, inc=1, device_id=device, device_id_type=MESH)

    fills = {}
    for k, (part, lo, hi) in enumerate((("e", 6, 8), ("e", 0, 2), ("c", 2, 4), ("d", 4, 6))):
        slots = LAST if k == 0 else FIRST if k == 1 else PARTS[part]
        fill = pltpu.make_async_copy(samples_ref.at[lo:hi], mine[0].at[slots], local_sem.at[k])
        fill.start()
        fills.setdefault(part, []).append(fill)
    scalars = [
        pltpu.make_async_copy(pairs_ref, pairs, local_sem.at[4]),
        pltpu.make_async_copy(bins_ref, bins, local_sem.at[5]),
    ]
    for copy in scalars:
        copy.start()

    barrier = pltpu.get_barrier_semaphore()
    greet(barrier, right)
    greet(barrier, left)
    pl.when(jnp.logical_not(first_core))(lambda: greet(barrier, other))
    pl.when(jnp.logical_not(turned_above))(lambda: greet(barrier, above))
    pl.when(turned_below)(lambda: greet(barrier, below))
    pl.semaphore_wait(
        barrier,
        2 + first_core.astype(jnp.int32) + turned_above.astype(jnp.int32)
        + jnp.logical_not(turned_below).astype(jnp.int32),
    )

    count = [0]
    sent = []

    def send(src, dst, device):
        k = count[0]
        count[0] += 1
        copy = pltpu.make_async_remote_copy(
            src_ref=src, dst_ref=dst, send_sem=send_sem.at[k], recv_sem=recv_sem.at[k],
            device_id=device, device_id_type=MESH,
        )
        copy.start()
        sent.append(copy)
        return copy

    ring = {}
    halos = {c: [] for c in range(chunks)}
    cross = {c: [] for c in range(chunks)}
    later = {"s": [], "u": [], "v": []}
    opened = set()

    def when_open(gate, act):
        if gate in opened:
            act()
        else:
            later[gate].append(act)

    def forward(step, part):
        here, there = of_step(step) if step else [0, 0], of_step(step + 1)
        cut = (slice(0, half), slice(half, rows)) if step + 1 == steps else (slice(0, rows),) * 2
        return [
            send(mine[here[k]].at[PARTS[part], cut[k]], mine[there[k]].at[PARTS[part]], (right, left)[k])
            for k in range(2)
        ]

    def arrive(part, step):
        if step == 0:
            for fill in fills[part]:
                fill.wait()
        else:
            for copy in ring[step - 1, part]:
                copy.wait_recv()
        if step < steps:
            ring[step, part] = forward(step, part)

        def to_neighbour(chunk, own, slots, device):
            halos[chunk].append(send(mine[chunk].at[own], mine[chunk].at[slots], device))

        for chunk in of_step(step):
            if part == "e":
                when_open("u", functools.partial(to_neighbour, chunk, LAST, FROM_BELOW, above))
                when_open("v", functools.partial(to_neighbour, chunk, FIRST, FROM_ABOVE, below))
            when_open("s", functools.partial(across, chunk, PARTS[part]))

    def across(chunk, slots):
        cross[chunk].append(send(mine[chunk].at[slots], theirs[chunk].at[slots], other))

    def open_gate(gate):
        if gate == "s":
            pl.when(jnp.logical_not(first_core))(lambda: pl.semaphore_wait(ready_sem.at[0], 1))
        elif gate == "u":
            pl.when(jnp.logical_not(turned_above))(lambda: pl.semaphore_wait(ready_sem.at[1], 1))
        else:
            pl.when(turned_below)(lambda: pl.semaphore_wait(ready_sem.at[2], 1))
        opened.add(gate)
        for act in later[gate]:
            act()

    start, band = t * 8, tiles * 8

    def load(step, put):
        for q in range(per_device):
            for side in range(2):
                slot = slot_of(pairs[side, p * per_device + q], start, band)
                row = 0
                for chunk in of_step(step):
                    for held in (mine[chunk], theirs[chunk]):
                        put(q, side, row, held[slot].astype(jnp.float32))
                        row += held.shape[1]

    def work(step):
        for chunk in of_step(step):
            for copy in cross[chunk]:
                copy.wait_recv()
        depth = sum(2 * mine[chunk].shape[1] for chunk in of_step(step))
        if step == 0:
            for copy in scalars:
                copy.wait()
            for q in range(per_device):
                weight = 1.0 - jnp.full((1, pixels), bins[0, q], jnp.int32).astype(jnp.float32) / NBINS
                factor_ref[q] = weight / jnp.float32(rows * group - 1)
            totals = {}

            def add(q, side, row, values):
                total = jnp.sum(values, axis=0, keepdims=True)
                totals[q, side] = total if row == 0 else totals[q, side] + total

            load(0, add)
            for (q, side), total in totals.items():
                shift_ref[2 * q + side] = (total * (1.0 / depth)).astype(jnp.bfloat16).astype(jnp.float32)
        final = step == steps
        sums = {}

        def put(q, side, row, values):
            u = (values - shift_ref[2 * q + side]).astype(jnp.bfloat16)
            into = last_ref if final else u_ref
            into[2 * q + side, pl.ds(row, values.shape[0]), :] = u
            total = jnp.sum(u.astype(jnp.float32), axis=0, keepdims=True)
            sums[q, side] = total if row == 0 else sums[q, side] + total

        load(step, put)
        for (q, side), total in sums.items():
            k = 2 * q + side
            sum_ref[k] = total if step == 0 else sum_ref[k] + total
        if final:
            return
        block = min(256, pixels)
        per_pair = pixels // block

        def body(i, _):
            q, m = lax.div(i, per_pair), pl.multiple_of(lax.rem(i, per_pair) * block, block)
            gram = lax.dot_general(
                u_ref[2 * q, 0:depth, pl.ds(m, block)], u_ref[2 * q + 1, 0:depth, :],
                (((0,), (0,)), ((), ())), preferred_element_type=jnp.float32,
            )
            if step == 0:
                acc_ref[q, pl.ds(m, block), :] = gram
            else:
                acc_ref[q, pl.ds(m, block), :] += gram
            return 0

        lax.fori_loop(0, per_device * per_pair, body, 0)

    first = True
    for what, step in schedule(steps):
        if what in PARTS:
            arrive(what, step)
        elif what == "x":
            for chunk in of_step(step):
                for copy in halos[chunk]:
                    copy.wait_recv()
                across(chunk, slice(FROM_BELOW.start, FROM_ABOVE.stop))
        elif what == "w":
            work(step)
        else:
            open_gate(what)
        if first:
            pl.when(first_core)(lambda: greet(ready_sem.at[0], other))
            pl.when(jnp.logical_not(turned_below))(lambda: greet(ready_sem.at[1], below))
            pl.when(turned_above)(lambda: greet(ready_sem.at[2], above))
            first = False
    for copy in sent:
        copy.wait_send()


def finish_kernel(plan, acc_ref, last_ref, sum_ref, factor_ref, out_ref, stage, sem):
    samples, pixels, per_device = plan
    block = min(256, pixels)
    copies = []
    for q in range(per_device):
        factor = factor_ref[q]
        total_a, total_b = sum_ref[2 * q], sum_ref[2 * q + 1] * (1.0 / samples)
        for m in range(0, pixels, block):
            rows = slice(m, m + block)
            gram = acc_ref[q, rows, :] + lax.dot_general(
                last_ref[2 * q, :, rows], last_ref[2 * q + 1], (((0,), (0,)), ((), ())),
                preferred_element_type=jnp.float32,
            )
            column = jnp.transpose(total_a[:, rows])
            stage[q, rows, :] = ((gram - column * total_b) * factor).astype(jnp.bfloat16)
            copy = pltpu.make_async_copy(stage.at[q, rows], out_ref.at[q, rows], sem.at[len(copies)])
            copy.start()
            copies.append(copy)
    for copy in copies:
        copy.wait()


def local(tiles, group, samples, pair_list, taper_bins):
    own_tiles, rows, pixels = samples.shape
    chips = group // 2
    steps = chips // 2
    per_device = taper_bins.shape[0]
    total_rows = rows * group
    plan = (tiles, chips, steps, rows, pixels, per_device)
    chunk_rows = [rows] * (2 * steps - 1) + [rows // 2] * 2
    chunks = [pltpu.VMEM((SLOTS, r, pixels), jnp.bfloat16) for r in chunk_rows]
    n_copies = 2 * 3 * steps + (2 + 4) * len(chunks)
    last_rows = 2 * rows
    acc, last, sums, factor = pl.pallas_call(
        functools.partial(gather_kernel, plan),
        out_shape=(
            pltpu.VMEM((per_device, pixels, pixels), jnp.float32),
            pltpu.VMEM((2 * per_device, last_rows, pixels), jnp.bfloat16),
            pltpu.VMEM((2 * per_device, 1, pixels), jnp.float32),
            pltpu.VMEM((per_device, 1, pixels), jnp.float32),
        ),
        in_specs=[pl.BlockSpec(memory_space=pl.ANY)] * 3,
        out_specs=[pl.BlockSpec(memory_space=pltpu.VMEM)] * 4,
        scratch_shapes=[
            *chunks,
            *chunks,
            pltpu.VMEM((2 * per_device, 4 * rows, pixels), jnp.bfloat16),
            pltpu.VMEM((2 * per_device, 1, pixels), jnp.float32),
            pltpu.SMEM((2, pair_list.shape[0]), jnp.int32),
            pltpu.SMEM((1, per_device), jnp.int32),
            pltpu.SemaphoreType.DMA((n_copies,)),
            pltpu.SemaphoreType.DMA((n_copies,)),
            pltpu.SemaphoreType.DMA((6,)),
            pltpu.SemaphoreType.REGULAR((3,)),
        ],
        compiler_params=pltpu.CompilerParams(
            collective_id=0, has_side_effects=True, vmem_limit_bytes=36 * 2**20
        ),
        name="gather_and_sum",
    )(*(pltpu.with_memory_space_constraint(v, pltpu.HBM) for v in (pair_list.T, taper_bins.reshape(1, -1), samples)))
    return pl.pallas_call(
        functools.partial(finish_kernel, (total_rows, pixels, per_device)),
        out_shape=jax.ShapeDtypeStruct((per_device, pixels, pixels), jnp.bfloat16),
        in_specs=[pl.BlockSpec(memory_space=pltpu.VMEM)] * 4,
        out_specs=pl.BlockSpec(memory_space=pl.ANY),
        scratch_shapes=[
            pltpu.VMEM((per_device, pixels, pixels), jnp.bfloat16),
            pltpu.SemaphoreType.DMA((per_device * max(1, pixels // 256),)),
        ],
        compiler_params=pltpu.CompilerParams(vmem_limit_bytes=36 * 2**20),
        name="finish",
    )(acc, last, sums, factor)


def solution(mesh):
    in_specs = (P("tile", "pair", None), P("tile", None), P(("tile", "pair")))
    out_specs = P(("tile", "pair"), None, None)
    body = functools.partial(local, mesh.shape["tile"], mesh.shape["pair"])
    return jax.shard_map(body, mesh=mesh, in_specs=in_specs, out_specs=out_specs, check_vma=False)
```

time: 72.4 us -> 59.4 us (0.82)
  Pallas kernels: 69.7 us -> 58.5 us
  local copies, waits for them, and re-layouts: 2.45 us -> 0 us
    pallas_call x1, Pallas kernels: 65.8 us -> 55.3 us  [local(): pl.pallas_call(functools.partial(gather_kernel, plan), out_shape=(pltpu.V...]
    unnamed x5 -> x0, local copies, waits for them, and re-layouts: 2.45 us -> none
    pallas_call x1, Pallas kernels: 3.92 us -> 3.16 us  [local(): pl.pallas_call(functools.partial(finish_kernel, (total_rows, pixels, per_...]
where the time goes in v2:
time: 59.4 us; the launch traced here: 58.5 us
  Pallas kernels  58.5 us (98%)
    pallas_call x1, Pallas kernels, local(): pl.pallas_call(functools.partial(gather_kernel, plan), out_shape=(pltpu.V...  55.3 us
    pallas_call x1, Pallas kernels, local(): pl.pallas_call(functools.partial(finish_kernel, (total_rows, pixels, per_...  3.16 us

profile of v2, /device:TPU:1, one launch (start us, length us, event | category | flops | bytes accessed | tf_op | source)
XLA Modules:
  0.0 58.5 jit_solution(9542544337598316189)
XLA Ops:
  0.0 55.3 %gather_and_sum.1 = (f32[2,1024,1024]{2,1,0:T(8,128)S(1)}, bf16[4,64,1024]{2,1,0:T(8,128)(2,1)S(1)}, f32[4,1,1024]{2,1,0:T(1,128)S(1)}, f32[2,1,1024]{2,1,0:T(1,128)S(1)}) custom-call(s32[2,32]{1,0:T(2,128)} %bitcast.2, s32[1,2]{1,0:T(1,128)} %bitcast.3, bf16[8,32,1024]{2,1,0:T(8,128)(2,1)} %samples_ref.1), custom_call_target="tpu_custom_call" | custom-call | tf_op jit(solution)/shard_map/gather_and_sum/pallas_call | solution.py:274
  55.3 3.2 %finish.1 = bf16[2,1024,1024]{2,1,0:T(8,128)(2,1)} custom-call(f32[2,1024,1024]{2,1,0:T(8,128)S(1)} %get-tuple-element.9.acc_ref, bf16[4,64,1024]{2,1,0:T(8,128)(2,1)S(1)} %get-tuple-element.10.last_ref, f32[4,1,1024]{2,1,0:T(1,128)S(1)} %get-tuple-element.11.sum_ref, f32[2,1,1024]{2,1,0:T(1,128)S(1)} %get-tuple-element.12.factor_ref), custom_call_target="tpu_custom_call" | custom-call | tf_op jit(solution)/shard_map/finish/pallas_call | solution.py:301

commit v3 on v2

v3 whole, which is shorter than its diff:
```python
import functools

import jax
import jax.numpy as jnp
from jax import lax
from jax.experimental import pallas as pl
from jax.experimental.pallas import tpu as pltpu
from jax.sharding import PartitionSpec as P

REACH = 2
NBINS = 8
LINE = 8
MESH = pl.DeviceIdType.MESH

INNER, ENDS, HALO = slice(0, 4), slice(4, 8), slice(8, 12)
LAST, FIRST = 4, 6
FROM_BELOW, FROM_ABOVE = 8, 10
SLOTS = 12
PIECES = 4
SPLIT_ROWS = 16


def schedule(steps):
    if steps == 4:
        text = (
            "p0 q0 i0 p1", "u0 q1 s0 p2", "i1 v0 x0 p3", "w0 q2 x1 i2", "p4 w1 A0 A1", "q3 A2 x2 A3",
            "w2 i3 x3 B0", "B1 B2 q4 w3", "B3 i4 x4 w4",
        )
    else:
        text = ("p0 q0 i0 p1", "u0 q1 s0 i1", "v0 x0 p2 w0", "A0 A1 A2 A3", "q2 x1 i2 x2", "w1 w2")
    return [(o[0], int(o[1:])) for line in text for o in line.split()]


def slot_of(tile, start, band):
    rel = jnp.clip(lax.rem(tile - start + REACH + band, band), 0, SLOTS - 1)
    return jnp.where(rel < 2, rel + 8, jnp.where(rel < 4, rel + 4, jnp.where(rel < 10, rel - 4, rel)))


def gather_kernel(plan, early, pairs_ref, bins_ref, samples_ref, acc_ref, last_ref, factor_ref, *scratch):
    tiles, chips, steps, rows, pixels, per_device = plan
    chunks = 2 * steps + 1
    mine, theirs = scratch[:chunks], scratch[chunks : 2 * chunks]
    sum_ref, u_ref, shift_ref, pairs, bins, send_sem, recv_sem, halo_send, halo_recv, local_sem, ready_sem = scratch[2 * chunks :]
    half = rows // 2

    def of_step(step):
        return [0] if step == 0 else [2 * step - 1, 2 * step]

    t, p = lax.axis_index("tile"), lax.axis_index("pair")
    group = 2 * chips
    core = lax.rem(p, 2)
    above, below = (lax.rem(t + 1, tiles), p), (lax.rem(t + tiles - 1, tiles), p)
    right, left = (t, lax.rem(p + 2, group)), (t, lax.rem(p + group - 2, group))
    other = (t, p + 1 - 2 * core)

    turned_below = lax.rem(t, LINE) == 0
    turned_above = lax.rem(lax.rem(t + 1, tiles), LINE) == 0
    first_core = core == 0

    lead = jnp.where(turned_above, LAST, FIRST)
    ends = {
        "p": (lead, jnp.where(turned_above, FROM_BELOW, FROM_ABOVE), turned_above),
        "q": (LAST + FIRST - lead, jnp.where(turned_above, FROM_ABOVE, FROM_BELOW), jnp.logical_not(turned_above)),
    }
    part_slots = {"p": pl.ds(ends["p"][0], 2), "q": pl.ds(ends["q"][0], 2), "i": INNER}

    def greet(sem, device):
        pl.semaphore_signal(sem, inc=1, device_id=device, device_id_type=MESH)

    fills = {}
    for k, (part, lo, hi) in enumerate((("p", 6, 8), ("p", 0, 2), ("i", 2, 6))):
        at = (LAST, FIRST, INNER.start)[k]
        fill = pltpu.make_async_copy(samples_ref.at[lo:hi], mine[0].at[at : at + hi - lo], local_sem.at[k])
        fill.start()
        fills.setdefault(part, []).append(fill)
    scalars = [
        pltpu.make_async_copy(pairs_ref, pairs, local_sem.at[3]),
        pltpu.make_async_copy(bins_ref, bins, local_sem.at[4]),
    ]
    for copy in scalars:
        copy.start()

    barrier = pltpu.get_barrier_semaphore()
    greet(barrier, right)
    greet(barrier, left)
    pl.when(jnp.logical_not(first_core))(lambda: greet(barrier, other))
    pl.when(jnp.logical_not(turned_above))(lambda: greet(barrier, above))
    pl.when(turned_below)(lambda: greet(barrier, below))
    pl.semaphore_wait(
        barrier,
        2 + first_core.astype(jnp.int32) + turned_above.astype(jnp.int32)
        + jnp.logical_not(turned_below).astype(jnp.int32),
    )

    count = [0]
    sent = []

    def send(src, dst, device):
        k = count[0]
        count[0] += 1
        copy = pltpu.make_async_remote_copy(
            src_ref=src, dst_ref=dst, send_sem=send_sem.at[k], recv_sem=recv_sem.at[k],
            device_id=device, device_id_type=MESH,
        )
        copy.start()
        sent.append(copy)
        return copy

    ring = {}
    cross = {c: [] for c in range(chunks)}
    later = {"s": [], "u": [], "v": []}
    opened = set()

    def forward(step, part):
        here, there = of_step(step) if step else [0, 0], of_step(step + 1)
        cut = (slice(0, half), slice(half, rows)) if step + 1 == steps else (slice(0, rows),) * 2
        slots = part_slots[part]
        return [
            send(mine[here[k]].at[slots, cut[k]], mine[there[k]].at[slots], (right, left)[k])
            for k in range(2)
        ]

    def halo(chunk, part):
        own, slots, up = ends[part]
        way = 1 - up.astype(jnp.int32)
        to = lax.rem(t + jnp.where(up, 1, tiles - 1), tiles)
        return pltpu.make_async_remote_copy(
            src_ref=mine[chunk].at[pl.ds(own, 2)], dst_ref=mine[chunk].at[pl.ds(slots, 2)],
            send_sem=halo_send.at[chunk, way], recv_sem=halo_recv.at[chunk, way],
            device_id=(to, p), device_id_type=MESH,
        )

    def halos_here(chunk, act):
        for way, (own, slots, device) in enumerate(((LAST, FROM_BELOW, above), (FIRST, FROM_ABOVE, below))):
            act(
                pltpu.make_async_remote_copy(
                    src_ref=mine[chunk].at[own : own + 2], dst_ref=mine[chunk].at[slots : slots + 2],
                    send_sem=halo_send.at[chunk, way], recv_sem=halo_recv.at[chunk, way],
                    device_id=device, device_id_type=MESH,
                )
            )

    def across(chunk, slots):
        if "s" in opened:
            cross[chunk].append(send(mine[chunk].at[slots], theirs[chunk].at[slots], other))
        else:
            later["s"].append((chunk, slots))

    def arrive(part, step):
        if step == 0:
            for fill in fills.get(part, ()):
                fill.wait()
        else:
            for copy in ring[step - 1, part]:
                copy.wait_recv()
        if step < steps:
            ring[step, part] = forward(step, part)
        for chunk in of_step(step):
            if part == "p":
                if "v" in opened:
                    halo(chunk, part).start()
                else:
                    pl.when(jnp.logical_not(turned_below))(lambda: halo(chunk, part).start())
                    later["v"].append(chunk)
            elif part == "q":
                if "u" in opened:
                    halo(chunk, part).start()
                else:
                    later["u"].append(chunk)
                across(chunk, ENDS)
            else:
                across(chunk, INNER)

    def open_gate(gate):
        opened.add(gate)
        if gate == "s":
            pl.when(jnp.logical_not(first_core))(lambda: pl.semaphore_wait(ready_sem.at[0], 1))
            for chunk, slots in later["s"]:
                across(chunk, slots)
        elif gate == "u":
            pl.when(jnp.logical_not(turned_above))(lambda: pl.semaphore_wait(ready_sem.at[1], 1))
            for chunk in later["u"]:
                halo(chunk, "q").start()
        else:

            @pl.when(turned_below)
            def _():
                pl.semaphore_wait(ready_sem.at[2], 1)
                for chunk in later["v"]:
                    halo(chunk, "p").start()

    start, band = t * 8, tiles * 8

    def load(step, put):
        for q in range(per_device):
            for side in range(2):
                slot = slot_of(pairs[side, p * per_device + q], start, band)
                row = 0
                for chunk in of_step(step):
                    for held in (mine[chunk], theirs[chunk]):
                        put(q, side, row, held[slot].astype(jnp.float32))
                        row += held.shape[1]

    def work(step):
        for chunk in of_step(step):
            for copy in cross[chunk]:
                copy.wait_recv()
        depth = sum(2 * mine[chunk].shape[1] for chunk in of_step(step))
        if step == 0:
            for copy in scalars:
                copy.wait()
            for q in range(per_device):
                weight = 1.0 - jnp.full((1, pixels), bins[0, q], jnp.int32).astype(jnp.float32) / NBINS
                factor_ref[q] = weight / jnp.float32(rows * group - 1)
            totals = {}

            def add(q, side, row, values):
                total = jnp.sum(values, axis=0, keepdims=True)
                totals[q, side] = total if row == 0 else totals[q, side] + total

            load(0, add)
            for (q, side), total in totals.items():
                shift_ref[2 * q + side] = (total * (1.0 / depth)).astype(jnp.bfloat16).astype(jnp.float32)
        final = step not in early
        into = last_ref if final else u_ref
        before = [n for n in range(step) if (n in early) == (not final)]
        first_row = sum(2 * mine[chunk].shape[1] for n in before for chunk in of_step(n))
        sums = {}

        def put(q, side, row, values):
            u = (values - shift_ref[2 * q + side]).astype(jnp.bfloat16)
            into[2 * q + side, pl.ds(first_row + row, values.shape[0]), :] = u
            total = jnp.sum(u.astype(jnp.float32), axis=0, keepdims=True)
            sums[q, side] = total if row == 0 else sums[q, side] + total

        load(step, put)
        for (q, side), total in sums.items():
            k = 2 * q + side
            total = total if step == 0 else sum_ref[k] + total
            if step < steps:
                sum_ref[k] = total
            else:
                total = total * (-1.0 / (rows * group)) if side == 0 else total
                high = total.astype(jnp.bfloat16).astype(jnp.float32)
                middle = (total - high).astype(jnp.bfloat16).astype(jnp.float32)
                low = total - high - middle
                row = lax.broadcasted_iota(jnp.int32, (SPLIT_ROWS, pixels), 0)
                is_middle = (row == 5) | (row == (2 if side == 0 else 1))
                is_low = row == (4 if side == 0 else 3)
                parts = jnp.where(row > 5, 0.0, jnp.where(is_middle, middle, jnp.where(is_low, low, high)))
                into[k, pl.ds(first_row + depth, SPLIT_ROWS), :] = parts.astype(jnp.bfloat16)

    def product(which, piece):
        cut = sum(2 * mine[chunk].shape[1] for n in early[:2] for chunk in of_step(n))
        from_rows = slice(0, cut) if which == "A" else slice(cut, u_ref.shape[1])
        block = per_device * pixels // PIECES
        q, m = divmod(piece * block, pixels)
        gram = lax.dot_general(
            u_ref[2 * q, from_rows, m : m + block], u_ref[2 * q + 1, from_rows, :],
            (((0,), (0,)), ((), ())), preferred_element_type=jnp.float32,
        )
        if which == "A":
            acc_ref[q, m : m + block, :] = gram
        else:
            acc_ref[q, m : m + block, :] += gram

    first = True
    for what, step in schedule(steps):
        if what in part_slots:
            arrive(what, step)
        elif what == "x":
            for chunk in of_step(step):
                halos_here(chunk, lambda copy: copy.wait_recv())
                across(chunk, HALO)
        elif what == "w":
            work(step)
        elif what in "AB":
            product(what, step)
        else:
            open_gate(what)
        if first:
            pl.when(first_core)(lambda: greet(ready_sem.at[0], other))
            pl.when(jnp.logical_not(turned_below))(lambda: greet(ready_sem.at[1], below))
            pl.when(turned_above)(lambda: greet(ready_sem.at[2], above))
            first = False
    for copy in sent:
        copy.wait_send()
    for chunk in range(chunks):
        halos_here(chunk, lambda copy: copy.wait_send())


def finish_kernel(acc_ref, last_ref, factor_ref, out_ref, stage, sem):
    per_device, pixels, _ = acc_ref.shape
    block = min(256, pixels)
    copies = []
    for q in range(per_device):
        for m in range(0, pixels, block):
            rows = slice(m, m + block)
            gram = acc_ref[q, rows, :] + lax.dot_general(
                last_ref[2 * q, :, rows], last_ref[2 * q + 1], (((0,), (0,)), ((), ())),
                preferred_element_type=jnp.float32,
            )
            stage[q, rows, :] = (gram * factor_ref[q]).astype(jnp.bfloat16)
            copy = pltpu.make_async_copy(stage.at[q, rows], out_ref.at[q, rows], sem.at[len(copies)])
            copy.start()
            copies.append(copy)
    for copy in copies:
        copy.wait()


def local(tiles, group, samples, pair_list, taper_bins):
    own_tiles, rows, pixels = samples.shape
    chips = group // 2
    steps = chips // 2
    per_device = taper_bins.shape[0]
    plan = (tiles, chips, steps, rows, pixels, per_device)
    chunk_rows = [rows] * (2 * steps - 1) + [rows // 2] * 2
    chunks = [pltpu.VMEM((SLOTS, r, pixels), jnp.bfloat16) for r in chunk_rows]
    n_copies = 2 * 3 * steps + 3 * len(chunks)
    early = list(range(steps - 1))
    early_rows = sum(2 * rows * (1 if n == 0 else 2) for n in early)
    last_rows = 2 * rows * chips - early_rows + SPLIT_ROWS
    acc, last, factor = pl.pallas_call(
        functools.partial(gather_kernel, plan, early),
        out_shape=(
            pltpu.VMEM((per_device, pixels, pixels), jnp.float32),
            pltpu.VMEM((2 * per_device, last_rows, pixels), jnp.bfloat16),
            pltpu.VMEM((per_device, 1, pixels), jnp.float32),
        ),
        in_specs=[pl.BlockSpec(memory_space=pl.ANY)] * 3,
        out_specs=[pl.BlockSpec(memory_space=pltpu.VMEM)] * 3,
        scratch_shapes=[
            *chunks,
            *chunks,
            pltpu.VMEM((2 * per_device, 1, pixels), jnp.float32),
            pltpu.VMEM((2 * per_device, early_rows, pixels), jnp.bfloat16),
            pltpu.VMEM((2 * per_device, 1, pixels), jnp.float32),
            pltpu.SMEM((2, pair_list.shape[0]), jnp.int32),
            pltpu.SMEM((1, per_device), jnp.int32),
            pltpu.SemaphoreType.DMA((n_copies,)),
            pltpu.SemaphoreType.DMA((n_copies,)),
            pltpu.SemaphoreType.DMA((len(chunks), 2)),
            pltpu.SemaphoreType.DMA((len(chunks), 2)),
            pltpu.SemaphoreType.DMA((5,)),
            pltpu.SemaphoreType.REGULAR((3,)),
        ],
        compiler_params=pltpu.CompilerParams(
            collective_id=0, has_side_effects=True, vmem_limit_bytes=36 * 2**20
        ),
        name="gather_and_sum",
    )(*(pltpu.with_memory_space_constraint(v, pltpu.HBM) for v in (pair_list.T, taper_bins.reshape(1, -1), samples)))
    return pl.pallas_call(
        finish_kernel,
        out_shape=jax.ShapeDtypeStruct((per_device, pixels, pixels), jnp.bfloat16),
        in_specs=[pl.BlockSpec(memory_space=pltpu.VMEM)] * 3,
        out_specs=pl.BlockSpec(memory_space=pl.ANY),
        scratch_shapes=[
            pltpu.VMEM((per_device, pixels, pixels), jnp.bfloat16),
            pltpu.SemaphoreType.DMA((per_device * max(1, pixels // 256),)),
        ],
        compiler_params=pltpu.CompilerParams(vmem_limit_bytes=36 * 2**20),
        name="finish",
    )(acc, last, factor)


def solution(mesh):
    in_specs = (P("tile", "pair", None), P("tile", None), P(("tile", "pair")))
    out_specs = P(("tile", "pair"), None, None)
    body = functools.partial(local, mesh.shape["tile"], mesh.shape["pair"])
    return jax.shard_map(body, mesh=mesh, in_specs=in_specs, out_specs=out_specs, check_vma=False)
```

time: 59.4 us -> 55.3 us (0.931); the launches traced: 58.5 us -> 55.2 us
  Pallas kernels: 58.5 us -> 55.2 us
    pallas_call x2, Pallas kernels: 58.5 us -> 55.2 us  [the longest x1 52.7 us: local(): pl.pallas_call(functools.partial(gather_kernel, plan, early), out_shape=(...]
where the time goes in v3:
time: 55.3 us; the launch traced here: 55.2 us
  Pallas kernels  55.2 us (100%)
    pallas_call x1, Pallas kernels, local(): pl.pallas_call(functools.partial(gather_kernel, plan, early), out_shape=(...  52.7 us
    pallas_call x1, Pallas kernels, local(): pl.pallas_call(finish_kernel, out_shape=jax.ShapeDtypeStruct((per_device,...  2.41 us

profile of v3, /device:TPU:1, one launch (start us, length us, event | category | flops | bytes accessed | tf_op | source)
XLA Modules:
  0.0 55.2 jit_solution(3432994117189302461)
XLA Ops:
  0.0 52.7 %gather_and_sum.1 = (f32[2,1024,1024]{2,1,0:T(8,128)S(1)}, bf16[4,208,1024]{2,1,0:T(8,128)(2,1)S(1)}, f32[2,1,1024]{2,1,0:T(1,128)S(1)}) custom-call(s32[2,32]{1,0:T(2,128)} %bitcast.2, s32[1,2]{1,0:T(1,128)} %bitcast.3, bf16[8,32,1024]{2,1,0:T(8,128)(2,1)} %samples_ref.1), custom_call_target="tpu_custom_call" | custom-call | tf_op jit(solution)/shard_map/gather_and_sum/pallas_call | solution.py:323
  52.8 2.4 %finish.1 = bf16[2,1024,1024]{2,1,0:T(8,128)(2,1)} custom-call(f32[2,1024,1024]{2,1,0:T(8,128)S(1)} %get-tuple-element.8.acc_ref, bf16[4,208,1024]{2,1,0:T(8,128)(2,1)S(1)} %get-tuple-element.9.last_ref, f32[2,1,1024]{2,1,0:T(1,128)S(1)} %get-tuple-element.10.factor_ref), custom_call_target="tpu_custom_call" | custom-call | tf_op jit(solution)/shard_map/finish/pallas_call | solution.py:352

commit v4 on v0

v4 whole, which is shorter than its diff:
```python
import functools

import jax
import jax.numpy as jnp
from jax import lax
from jax.experimental import pallas as pl
from jax.experimental.pallas import tpu as pltpu
from jax.sharding import PartitionSpec as P

REACH = 2
NBINS = 8
LINE = 8
MESH = pl.DeviceIdType.MESH

INNER, ENDS, HALO = slice(0, 4), slice(4, 8), slice(8, 12)
LAST, FIRST = 4, 6
FROM_BELOW, FROM_ABOVE = 8, 10
SLOTS = 12
PIECES = 4
SPLIT_ROWS = 16


def schedule(steps, bottom):
    if steps != 4:
        text = (
            "p0 q0 i0 p1", "u0 q1 s0 i1", "v0 x0 p2 w0", "A0 A1 A2 A3",
            "q2 x1 w1 x2", "i2 m2 w2 y0", "h0 h1",
        )
    elif bottom:
        text = (
            "p0 q0 i0 p1", "u0 q1 s0 i1", "v0 p2 q2 x0", "i2 x1 w0 p3",
            "w1 q3 A0 A1", "x2 A2 A3 i3", "w2 B0 B1 p4", "x3 q4 B2 B3",
            "w3 x4 i4 m4", "w4 y0 h0 h1", "h2 h3",
        )
    else:
        text = (
            "p0 q0 p1 i0", "u0 s0 p2 q1", "p3 v0 i1 x0", "w0 p4 q2 x1",
            "i2 w1 A0 A1", "q3 x2 A2 A3", "i3 w2 B0 B1", "x3 B2 B3 q4",
            "w3 x4 i4 m4", "w4 y0 h0 h1", "h2 h3",
        )
    return [(o[0], int(o[1:])) for line in text for o in line.split()]


def slot_of(tile, start, band):
    rel = jnp.clip(lax.rem(tile - start + REACH + band, band), 0, SLOTS - 1)
    return jnp.where(rel < 2, rel + 8, jnp.where(rel < 4, rel + 4, jnp.where(rel < 10, rel - 4, rel)))


def gather_kernel(plan, early, pairs_ref, bins_ref, samples_ref, acc_ref, last_ref, factor_ref, *scratch):
    tiles, chips, steps, rows, pixels, per_device = plan
    chunks = 2 * steps + 1
    mine, theirs = scratch[:chunks], scratch[chunks : 2 * chunks]
    sum_ref, u_ref, shift_ref, pairs, bins, send_sem, recv_sem, halo_send, halo_recv, local_sem, ready_sem = scratch[2 * chunks :]
    half = rows // 2

    def of_step(step):
        return [0] if step == 0 else [2 * step - 1, 2 * step]

    t, p = lax.axis_index("tile"), lax.axis_index("pair")
    group = 2 * chips
    core = lax.rem(p, 2)
    above, below = (lax.rem(t + 1, tiles), p), (lax.rem(t + tiles - 1, tiles), p)
    right, left = (t, lax.rem(p + 2, group)), (t, lax.rem(p + group - 2, group))
    other = (t, p + 1 - 2 * core)

    turned_below = lax.rem(t, LINE) == 0
    turned_above = lax.rem(lax.rem(t + 1, tiles), LINE) == 0
    first_core = core == 0

    lead = jnp.where(turned_above, LAST, FIRST)
    ends = {
        "p": (lead, jnp.where(turned_above, FROM_BELOW, FROM_ABOVE), turned_above),
        "q": (LAST + FIRST - lead, jnp.where(turned_above, FROM_ABOVE, FROM_BELOW), jnp.logical_not(turned_above)),
    }
    part_slots = {"p": pl.ds(ends["p"][0], 2), "q": pl.ds(ends["q"][0], 2), "i": INNER}

    def greet(sem, device):
        pl.semaphore_signal(sem, inc=1, device_id=device, device_id_type=MESH)

    barrier = pltpu.get_barrier_semaphore()
    greet(barrier, right)
    greet(barrier, left)
    pl.when(jnp.logical_not(first_core))(lambda: greet(barrier, other))
    pl.when(jnp.logical_not(turned_above))(lambda: greet(barrier, above))
    pl.when(turned_below)(lambda: greet(barrier, below))
    fills = {}
    for k, (part, lo, hi) in enumerate((("p", 6, 8), ("p", 0, 2), ("i", 2, 6))):
        at = (LAST, FIRST, INNER.start)[k]
        fill = pltpu.make_async_copy(samples_ref.at[lo:hi], mine[0].at[at : at + hi - lo], local_sem.at[k])
        fill.start()
        fills.setdefault(part, []).append(fill)
    scalars = [
        pltpu.make_async_copy(pairs_ref, pairs, local_sem.at[3]),
        pltpu.make_async_copy(bins_ref, bins, local_sem.at[4]),
    ]
    for copy in scalars:
        copy.start()

    pl.semaphore_wait(
        barrier,
        2 + first_core.astype(jnp.int32) + turned_above.astype(jnp.int32)
        + jnp.logical_not(turned_below).astype(jnp.int32),
    )

    def run(order):
        count = [0]
        sent = []

        def send(src, dst, device):
            k = count[0]
            count[0] += 1
            copy = pltpu.make_async_remote_copy(
                src_ref=src, dst_ref=dst, send_sem=send_sem.at[k], recv_sem=recv_sem.at[k],
                device_id=device, device_id_type=MESH,
            )
            copy.start()
            sent.append(copy)
            return copy

        ring = {}
        cross = {c: [] for c in range(chunks)}
        later = {"s": [], "u": [], "v": []}
        opened = set()

        def forward(step, part, k):
            here = of_step(step)[k] if step else 0
            there = of_step(step + 1)[k]
            cut = (slice(0, half), slice(half, rows))[k] if step + 1 == steps else slice(0, rows)
            slots = part_slots[part]
            return send(mine[here].at[slots, cut], mine[there].at[slots], (right, left)[k])

        def halo(chunk, part):
            own, slots, up = ends[part]
            way = 1 - up.astype(jnp.int32)
            to = lax.rem(t + jnp.where(up, 1, tiles - 1), tiles)
            return pltpu.make_async_remote_copy(
                src_ref=mine[chunk].at[pl.ds(own, 2)], dst_ref=mine[chunk].at[pl.ds(slots, 2)],
                send_sem=halo_send.at[chunk, way], recv_sem=halo_recv.at[chunk, way],
                device_id=(to, p), device_id_type=MESH,
            )

        def halos_here(chunk, act):
            for way, (own, slots, device) in enumerate(((LAST, FROM_BELOW, above), (FIRST, FROM_ABOVE, below))):
                act(
                    pltpu.make_async_remote_copy(
                        src_ref=mine[chunk].at[own : own + 2], dst_ref=mine[chunk].at[slots : slots + 2],
                        send_sem=halo_send.at[chunk, way], recv_sem=halo_recv.at[chunk, way],
                        device_id=device, device_id_type=MESH,
                    )
                )

        def across(chunk, slots):
            if "s" in opened:
                cross[chunk].append(send(mine[chunk].at[slots], theirs[chunk].at[slots], other))
            else:
                later["s"].append((chunk, slots))

        def arrive(part, step):
            if step == 0:
                for fill in fills.get(part, ()):
                    fill.wait()
            ring[step, part] = []
            for k in range(2):
                if step > 0:
                    ring[step - 1, part][k].wait_recv()
                if step < steps:
                    ring[step, part].append(forward(step, part, k))
            for chunk in of_step(step):
                if part == "p":
                    if "v" in opened:
                        halo(chunk, part).start()
                    else:
                        pl.when(jnp.logical_not(turned_below))(lambda: halo(chunk, part).start())
                        later["v"].append(chunk)
                elif part == "q":
                    if "u" in opened:
                        halo(chunk, part).start()
                    else:
                        later["u"].append(chunk)
                    across(chunk, ENDS)
                else:
                    across(chunk, INNER)

        def open_gate(gate):
            opened.add(gate)
            if gate == "s":
                pl.when(jnp.logical_not(first_core))(lambda: pl.semaphore_wait(ready_sem.at[0], 1))
                for chunk, slots in later["s"]:
                    across(chunk, slots)
            elif gate == "u":
                pl.when(jnp.logical_not(turned_above))(lambda: pl.semaphore_wait(ready_sem.at[1], 1))
                for chunk in later["u"]:
                    halo(chunk, "q").start()
            else:

                @pl.when(turned_below)
                def _():
                    pl.semaphore_wait(ready_sem.at[2], 1)
                    for chunk in later["v"]:
                        halo(chunk, "p").start()

        start, band = t * 8, tiles * 8

        def load(step, put, cores):
            for q in range(per_device):
                for side in range(2):
                    slot = slot_of(pairs[side, p * per_device + q], start, band)
                    row = 0
                    for n, core_chunks in enumerate((mine, theirs)):
                        for chunk in of_step(step):
                            held = core_chunks[chunk]
                            if n in cores:
                                put(q, side, row, held[slot].astype(jnp.float32))
                            row += held.shape[1]

        def work(step, cores=(0, 1)):
            if 1 in cores:
                for chunk in of_step(step):
                    for copy in cross[chunk]:
                        copy.wait_recv()
            depth = sum(2 * mine[chunk].shape[1] for chunk in of_step(step))
            if step == 0:
                for copy in scalars:
                    copy.wait()
                for q in range(per_device):
                    weight = 1.0 - jnp.full((1, pixels), bins[0, q], jnp.int32).astype(jnp.float32) / NBINS
                    factor_ref[q] = weight / jnp.float32(rows * group - 1)
                totals = {}

                def add(q, side, row, values):
                    total = jnp.sum(values, axis=0, keepdims=True)
                    totals[q, side] = total if row == 0 else totals[q, side] + total

                load(0, add, cores)
                for (q, side), total in totals.items():
                    shift_ref[2 * q + side] = (total * (1.0 / depth)).astype(jnp.bfloat16).astype(jnp.float32)
            final = step not in early
            into = last_ref if final else u_ref
            before = [n for n in range(step) if (n in early) == (not final)]
            first_row = sum(2 * mine[chunk].shape[1] for n in before for chunk in of_step(n))
            sums = {}

            def put(q, side, row, values):
                u = (values - shift_ref[2 * q + side]).astype(jnp.bfloat16)
                into[2 * q + side, pl.ds(first_row + row, values.shape[0]), :] = u
                total = jnp.sum(u.astype(jnp.float32), axis=0, keepdims=True)
                sums[q, side] = sums[q, side] + total if (q, side) in sums else total

            load(step, put, cores)
            for (q, side), total in sums.items():
                k = 2 * q + side
                total = total if step == 0 else sum_ref[k] + total
                if step < steps or 1 not in cores:
                    sum_ref[k] = total
                else:
                    total = total * (-1.0 / (rows * group)) if side == 0 else total
                    high = total.astype(jnp.bfloat16).astype(jnp.float32)
                    middle = (total - high).astype(jnp.bfloat16).astype(jnp.float32)
                    low = total - high - middle
                    row = lax.broadcasted_iota(jnp.int32, (SPLIT_ROWS, pixels), 0)
                    is_middle = (row == 5) | (row == (2 if side == 0 else 1))
                    is_low = row == (4 if side == 0 else 3)
                    parts = jnp.where(row > 5, 0.0, jnp.where(is_middle, middle, jnp.where(is_low, low, high)))
                    into[k, pl.ds(first_row + depth, SPLIT_ROWS), :] = parts.astype(jnp.bfloat16)

        state = [0, 0]

        def drain():
            done, mark = state
            for copy in sent[done:mark]:
                copy.wait_send()
            state[:] = mark, len(sent)

        def drain_halos(step):
            for chunk in of_step(step):
                halos_here(chunk, lambda copy: copy.wait_send())

        def product(which, piece):
            cut = sum(2 * mine[chunk].shape[1] for n in early[:2] for chunk in of_step(n))
            from_rows = slice(0, cut) if which == "A" else slice(cut, u_ref.shape[1])
            block = per_device * pixels // PIECES
            q, m = divmod(piece * block, pixels)
            gram = lax.dot_general(
                u_ref[2 * q, from_rows, m : m + block], u_ref[2 * q + 1, from_rows, :],
                (((0,), (0,)), ((), ())), preferred_element_type=jnp.float32,
            )
            if which == "A":
                acc_ref[q, m : m + block, :] = gram
            else:
                acc_ref[q, m : m + block, :] += gram

        first = True
        for what, step in order:
            if what in part_slots:
                arrive(what, step)
            elif what == "x":
                for chunk in of_step(step):
                    halos_here(chunk, lambda copy: copy.wait_recv())
                    across(chunk, HALO)
            elif what == "m":
                work(step, (0,))
            elif what == "w":
                work(step, (1,) if step == steps else (0, 1))
            elif what == "y":
                drain()
            elif what == "h":
                drain_halos(step)
            elif what in "AB":
                product(what, step)
            else:
                open_gate(what)
            if first:
                pl.when(first_core)(lambda: greet(ready_sem.at[0], other))
                pl.when(jnp.logical_not(turned_below))(lambda: greet(ready_sem.at[1], below))
                pl.when(turned_above)(lambda: greet(ready_sem.at[2], above))
                first = False
        drain()
        drain()
        drain_halos(steps)

    pl.when(turned_below)(lambda: run(schedule(steps, True)))
    pl.when(jnp.logical_not(turned_below))(lambda: run(schedule(steps, False)))


def finish_kernel(acc_ref, last_ref, factor_ref, out_ref, stage, sem):
    per_device, pixels, _ = acc_ref.shape
    block = min(256, pixels)
    copies = []
    for q in range(per_device):
        for m in range(0, pixels, block):
            rows = slice(m, m + block)
            gram = acc_ref[q, rows, :] + lax.dot_general(
                last_ref[2 * q, :, rows], last_ref[2 * q + 1], (((0,), (0,)), ((), ())),
                preferred_element_type=jnp.float32,
            )
            stage[q, rows, :] = (gram * factor_ref[q]).astype(jnp.bfloat16)
            copy = pltpu.make_async_copy(stage.at[q, rows], out_ref.at[q, rows], sem.at[len(copies)])
            copy.start()
            copies.append(copy)
    for copy in copies:
        copy.wait()


def local(tiles, group, samples, pair_list, taper_bins):
    own_tiles, rows, pixels = samples.shape
    chips = group // 2
    steps = chips // 2
    per_device = taper_bins.shape[0]
    plan = (tiles, chips, steps, rows, pixels, per_device)
    chunk_rows = [rows] * (2 * steps - 1) + [rows // 2] * 2
    chunks = [pltpu.VMEM((SLOTS, r, pixels), jnp.bfloat16) for r in chunk_rows]
    n_copies = 2 * 3 * steps + 3 * len(chunks)
    early = list(range(steps - 1))
    early_rows = sum(2 * rows * (1 if n == 0 else 2) for n in early)
    last_rows = 2 * rows * chips - early_rows + SPLIT_ROWS
    acc, last, factor = pl.pallas_call(
        functools.partial(gather_kernel, plan, early),
        out_shape=(
            pltpu.VMEM((per_device, pixels, pixels), jnp.float32),
            pltpu.VMEM((2 * per_device, last_rows, pixels), jnp.bfloat16),
            pltpu.VMEM((per_device, 1, pixels), jnp.float32),
        ),
        in_specs=[pl.BlockSpec(memory_space=pl.ANY)] * 3,
        out_specs=[pl.BlockSpec(memory_space=pltpu.VMEM)] * 3,
        scratch_shapes=[
            *chunks,
            *chunks,
            pltpu.VMEM((2 * per_device, 1, pixels), jnp.float32),
            pltpu.VMEM((2 * per_device, early_rows, pixels), jnp.bfloat16),
            pltpu.VMEM((2 * per_device, 1, pixels), jnp.float32),
            pltpu.SMEM((2, pair_list.shape[0]), jnp.int32),
            pltpu.SMEM((1, per_device), jnp.int32),
            pltpu.SemaphoreType.DMA((n_copies,)),
            pltpu.SemaphoreType.DMA((n_copies,)),
            pltpu.SemaphoreType.DMA((len(chunks), 2)),
            pltpu.SemaphoreType.DMA((len(chunks), 2)),
            pltpu.SemaphoreType.DMA((5,)),
            pltpu.SemaphoreType.REGULAR((3,)),
        ],
        compiler_params=pltpu.CompilerParams(
            collective_id=0, has_side_effects=True, vmem_limit_bytes=36 * 2**20
        ),
        name="gather_and_sum",
    )(*(pltpu.with_memory_space_constraint(v, pltpu.HBM) for v in (pair_list.T, taper_bins.reshape(1, -1), samples)))
    return pl.pallas_call(
        finish_kernel,
        out_shape=jax.ShapeDtypeStruct((per_device, pixels, pixels), jnp.bfloat16),
        in_specs=[pl.BlockSpec(memory_space=pltpu.VMEM)] * 3,
        out_specs=pl.BlockSpec(memory_space=pl.ANY),
        scratch_shapes=[
            pltpu.VMEM((per_device, pixels, pixels), jnp.bfloat16),
            pltpu.SemaphoreType.DMA((per_device * max(1, pixels // 256),)),
        ],
        compiler_params=pltpu.CompilerParams(vmem_limit_bytes=36 * 2**20),
        name="finish",
    )(acc, last, factor)


def solution(mesh):
    in_specs = (P("tile", "pair", None), P("tile", None), P(("tile", "pair")))
    out_specs = P(("tile", "pair"), None, None)
    body = functools.partial(local, mesh.shape["tile"], mesh.shape["pair"])
    return jax.shard_map(body, mesh=mesh, in_specs=in_specs, out_specs=out_specs, check_vma=False)
```

time: 177 us -> 54 us (0.31)
  the two profiles are of different devices: /device:TPU:1 before, /device:TPU:389 now
where the time goes in v4:
time: 54 us; the launch traced here: 53.9 us
  Pallas kernels  53.9 us (100%)
    pallas_call x1, Pallas kernels, local(): pl.pallas_call(functools.partial(gather_kernel, plan, early), out_shape=(...  51.5 us
    pallas_call x1, Pallas kernels, local(): pl.pallas_call(finish_kernel, out_shape=jax.ShapeDtypeStruct((per_device,...  2.41 us

profile of v4, /device:TPU:389, one launch (start us, length us, event | category | flops | bytes accessed | tf_op | source)
XLA Modules:
  0.0 53.9 jit_solution(13931213736725002951)
XLA Ops:
  0.0 51.5 %gather_and_sum.1 = (f32[2,1024,1024]{2,1,0:T(8,128)S(1)}, bf16[4,208,1024]{2,1,0:T(8,128)(2,1)S(1)}, f32[2,1,1024]{2,1,0:T(1,128)S(1)}) custom-call(s32[2,32]{1,0:T(2,128)} %bitcast.2, s32[1,2]{1,0:T(1,128)} %bitcast.3, bf16[8,32,1024]{2,1,0:T(8,128)(2,1)} %samples_ref.1), custom_call_target="tpu_custom_call" | custom-call | tf_op jit(solution)/shard_map/gather_and_sum/pallas_call | solution.py:356
  51.5 2.4 %finish.1 = bf16[2,1024,1024]{2,1,0:T(8,128)(2,1)} custom-call(f32[2,1024,1024]{2,1,0:T(8,128)S(1)} %get-tuple-element.8.acc_ref, bf16[4,208,1024]{2,1,0:T(8,128)(2,1)S(1)} %get-tuple-element.9.last_ref, f32[2,1,1024]{2,1,0:T(1,128)S(1)} %get-tuple-element.10.factor_ref), custom_call_target="tpu_custom_call" | custom-call | tf_op jit(solution)/shard_map/finish/pallas_call | solution.py:385

commit v5 on v4

--- a/solution.py
+++ b/solution.py
@@ -34,9 +34,9 @@
         )
     else:
         text = (
-            "p0 q0 p1 i0", "u0 s0 p2 q1", "p3 v0 i1 x0", "w0 p4 q2 x1",
-            "i2 w1 A0 A1", "q3 x2 A2 A3", "i3 w2 B0 B1", "x3 B2 B3 q4",
-            "w3 x4 i4 m4", "w4 y0 h0 h1", "h2 h3",
+            "p0 q0 c0 p1", "u0 s0 c1 p2", "q1 p3 d0 v0", "q2 x0 d1 p4",
+            "w0 q3 x1 c2", "w1 A0 A1 d2", "q4 x2 A2 A3", "c3 w2 B0 B1",
+            "d3 x3 B2 B3", "w3 x4 c4 d4", "m4 w4 y0 h0", "h1 h2 h3",
         )
     return [(o[0], int(o[1:])) for line in text for o in line.split()]
 
@@ -72,7 +72,7 @@
         "p": (lead, jnp.where(turned_above, FROM_BELOW, FROM_ABOVE), turned_above),
         "q": (LAST + FIRST - lead, jnp.where(turned_above, FROM_ABOVE, FROM_BELOW), jnp.logical_not(turned_above)),
     }
-    part_slots = {"p": pl.ds(ends["p"][0], 2), "q": pl.ds(ends["q"][0], 2), "i": INNER}
+    part_slots = {"p": pl.ds(ends["p"][0], 2), "q": pl.ds(ends["q"][0], 2), "i": INNER, "c": slice(0, 2), "d": slice(2, 4)}
 
     def greet(sem, device):
         pl.semaphore_signal(sem, inc=1, device_id=device, device_id_type=MESH)
@@ -157,7 +157,7 @@
 
         def arrive(part, step):
             if step == 0:
-                for fill in fills.get(part, ()):
+                for fill in fills.get("i" if part == "c" else part, ()):
                     fill.wait()
             ring[step, part] = []
             for k in range(2):
@@ -179,7 +179,7 @@
                         later["u"].append(chunk)
                     across(chunk, ENDS)
                 else:
-                    across(chunk, INNER)
+                    across(chunk, part_slots[part])
 
         def open_gate(gate):
             opened.add(gate)
@@ -349,7 +349,7 @@
     plan = (tiles, chips, steps, rows, pixels, per_device)
     chunk_rows = [rows] * (2 * steps - 1) + [rows // 2] * 2
     chunks = [pltpu.VMEM((SLOTS, r, pixels), jnp.bfloat16) for r in chunk_rows]
-    n_copies = 2 * 3 * steps + 3 * len(chunks)
+    n_copies = 2 * 4 * steps + 4 * len(chunks)
     early = list(range(steps - 1))
     early_rows = sum(2 * rows * (1 if n == 0 else 2) for n in early)
     last_rows = 2 * rows * chips - early_rows + SPLIT_ROWS

time: 54 us -> 53.3 us (0.987)
  the two profiles are of different devices: /device:TPU:389 before, /device:TPU:1 now
where the time goes in v5:
time: 53.3 us; the launch traced here: 53.1 us
  Pallas kernels  53.1 us (100%)
    pallas_call x1, Pallas kernels, local(): pl.pallas_call(functools.partial(gather_kernel, plan, early), out_shape=(...  50.7 us
    pallas_call x1, Pallas kernels, local(): pl.pallas_call(finish_kernel, out_shape=jax.ShapeDtypeStruct((per_device,...  2.4 us

profile of v5, /device:TPU:1, one launch (start us, length us, event | category | flops | bytes accessed | tf_op | source)
XLA Modules:
  0.0 53.1 jit_solution(18185321091723407781)
XLA Ops:
  0.0 50.7 %gather_and_sum.1 = (f32[2,1024,1024]{2,1,0:T(8,128)S(1)}, bf16[4,208,1024]{2,1,0:T(8,128)(2,1)S(1)}, f32[2,1,1024]{2,1,0:T(1,128)S(1)}) custom-call(s32[2,32]{1,0:T(2,128)} %bitcast.2, s32[1,2]{1,0:T(1,128)} %bitcast.3, bf16[8,32,1024]{2,1,0:T(8,128)(2,1)} %samples_ref.1), custom_call_target="tpu_custom_call" | custom-call | tf_op jit(solution)/shard_map/gather_and_sum/pallas_call | solution.py:356
  50.7 2.4 %finish.1 = bf16[2,1024,1024]{2,1,0:T(8,128)(2,1)} custom-call(f32[2,1024,1024]{2,1,0:T(8,128)S(1)} %get-tuple-element.8.acc_ref, bf16[4,208,1024]{2,1,0:T(8,128)(2,1)S(1)} %get-tuple-element.9.last_ref, f32[2,1,1024]{2,1,0:T(1,128)S(1)} %get-tuple-element.10.factor_ref), custom_call_target="tpu_custom_call" | custom-call | tf_op jit(solution)/shard_map/finish/pallas_call | solution.py:385

commit v6 on v5

--- a/solution.py
+++ b/solution.py
@@ -28,9 +28,9 @@
         )
     elif bottom:
         text = (
-            "p0 q0 i0 p1", "u0 q1 s0 i1", "v0 p2 q2 x0", "i2 x1 w0 p3",
-            "w1 q3 A0 A1", "x2 A2 A3 i3", "w2 B0 B1 p4", "x3 q4 B2 B3",
-            "w3 x4 i4 m4", "w4 y0 h0 h1", "h2 h3",
+            "p0 q0 c0 d0", "p1 u0 q1 s0", "c1 d1 v0 p2", "q2 x0 c2 d2",
+            "x1 w0 p3 w1", "q3 A0 A1 x2", "A2 A3 c3 d3", "w2 B0 B1 p4",
+            "x3 q4 B2 B3", "w3 x4 c4 d4", "m4 w4 y0 h0", "h1 h2 h3",
         )
     else:
         text = (

time: 53.3 us -> 52.9 us (level)
  Pallas kernels: 53.1 us -> 52.5 us
    pallas_call x1, Pallas kernels: 50.7 us -> 50.1 us  [local(): pl.pallas_call(functools.partial(gather_kernel, plan, early), out_shape=(...]
where the time goes in v6:
time: 52.9 us; the launch traced here: 52.5 us
  Pallas kernels  52.5 us (99%)
    pallas_call x1, Pallas kernels, local(): pl.pallas_call(functools.partial(gather_kernel, plan, early), out_shape=(...  50.1 us
    pallas_call x1, Pallas kernels, local(): pl.pallas_call(finish_kernel, out_shape=jax.ShapeDtypeStruct((per_device,...  2.41 us

profile of v6, /device:TPU:1, one launch (start us, length us, event | category | flops | bytes accessed | tf_op | source)
XLA Modules:
  0.0 52.5 jit_solution(11642434370754685445)
XLA Ops:
  0.0 50.1 %gather_and_sum.1 = (f32[2,1024,1024]{2,1,0:T(8,128)S(1)}, bf16[4,208,1024]{2,1,0:T(8,128)(2,1)S(1)}, f32[2,1,1024]{2,1,0:T(1,128)S(1)}) custom-call(s32[2,32]{1,0:T(2,128)} %bitcast.2, s32[1,2]{1,0:T(1,128)} %bitcast.3, bf16[8,32,1024]{2,1,0:T(8,128)(2,1)} %samples_ref.1), custom_call_target="tpu_custom_call" | custom-call | tf_op jit(solution)/shard_map/gather_and_sum/pallas_call | solution.py:356
  50.1 2.4 %finish.1 = bf16[2,1024,1024]{2,1,0:T(8,128)(2,1)} custom-call(f32[2,1024,1024]{2,1,0:T(8,128)S(1)} %get-tuple-element.8.acc_ref, bf16[4,208,1024]{2,1,0:T(8,128)(2,1)S(1)} %get-tuple-element.9.last_ref, f32[2,1,1024]{2,1,0:T(1,128)S(1)} %get-tuple-element.10.factor_ref), custom_call_target="tpu_custom_call" | custom-call | tf_op jit(solution)/shard_map/finish/pallas_call | solution.py:385
